TPU v7x, 32 devices: a whole 2x2x4 slice. The times are simulated.
32 devices in a mesh: dom: 32 (over z, y, x, core).
Axes of the slice: x: 2, y: 2, z: 4, core: 2. Of those that a mesh axis runs over, the one named last changes fastest.
Arguments:
- blocks: bfloat16 [4096, 128, 128], P('dom'), may hold values from 2.4e-05 to 0.161
- col_index: int32 [32, 128], P('dom'), may hold values from 0 to 79, as said below
- row_offsets: int32 [32, 33], P('dom'), may hold values from 0 to 128, as said below
- send_index: int32 [32, 6, 8], P('dom'), may hold values from 0 to 31, as said below
- deg_scale: float32 [131072], P('dom'), may hold values from 0.5 to 1
- seeds: float32 [16, 131072], P(None, 'dom'), may hold values from 0.25 to 2
Outputs:
- spread: float32 [16, 131072], P(None, 'dom')
Inputs may be any that keep to these rules, and one draw needn't show every extreme that they name: In every partition the offsets start at 0 and rise by 1 to 4 per block row; slots from row_offsets[p, 32] on are unused; some partition uses all 128 slots. `col_index`: the first slot of block row r names the partition's own block r; entries below 32 name own blocks, the others received blocks. `send_index`: each list names 8 distinct blocks of the sending partition; its six lists together name every one of its blocks.
All inputs are finite; a program needn't handle non-finite values.
Results may differ from a plain program's by a relative error of at most 0.0003.
Values may be sent and summed in bfloat16 or wider, within the bound.
A program may use at most 64 MiB of HBM per device.

v0:
```python
import jax
import jax.numpy as jnp
from jax import lax
from jax.sharding import PartitionSpec as P

ITERS = 4


OFFSETS = (1, -1, 2, -2, 4, -4)
ALPHA = 0.8


def passed_along(x, axis, by):
    count = lax.axis_size(axis)
    return lax.ppermute(x, axis, [(i, (i + by) % count) for i in range(count)])


def on_device(blocks, col_index, row_offsets, send_index, deg_scale, seeds):
    blk = blocks.shape[1]
    width = seeds.shape[0]
    nrb = deg_scale.shape[0] // blk
    columns = col_index[0]
    offsets = row_offsets[0]
    lists = send_index[0]
    slots = jnp.arange(blocks.shape[0], dtype=jnp.int32)
    row_of = jnp.sum((offsets[1:, None] <= slots[None, :]).astype(jnp.int32), axis=0)
    onehot = (row_of[None, :] == jnp.arange(nrb, dtype=jnp.int32)[:, None]).astype(jnp.float32)
    scale = deg_scale.reshape(1, nrb, blk)
    base = seeds.reshape(width, nrb, blk)
    theirs = []
    for j in range(2):
        theirs.append(passed_along(lists[j], "dom", OFFSETS[j]))
    for j in range(2, 6):
        theirs.append(passed_along(lists[j], "dom", OFFSETS[j]))
    field = base
    for step in range(ITERS):
        scaled = (field * scale).astype(jnp.bfloat16)
        pieces = [scaled]
        for j in range(2):
            pieces.append(passed_along(scaled, "dom", OFFSETS[j])[:, theirs[j]])
        for j in range(2, 6):
            pieces.append(passed_along(scaled, "dom", OFFSETS[j])[:, theirs[j]])
        extended = jnp.concatenate(pieces, axis=1)
        picked = extended[:, columns]
        prods = jnp.einsum("ckj,kij->kci", picked, blocks, preferred_element_type=jnp.float32)
        summed = jnp.einsum("rk,kci->cri", onehot, prods, precision=lax.Precision.HIGHEST)
        field = ALPHA * scale * summed + (1.0 - ALPHA) * base
    return field.reshape(width, nrb * blk)


def solution(mesh):
    in_specs = (
        P("dom", None, None),
        P("dom", None),
        P("dom", None),
        P("dom", None, None),
        P("dom"),
        P(None, "dom"),
    )
    out_specs = P(None, "dom")
    return jax.shard_map(
        on_device, mesh=mesh, in_specs=in_specs, out_specs=out_specs, check_vma=False
    )
```

profile of v0, /device:TPU:0, one launch (start us, length us, event | category | flops | bytes accessed | tf_op | source)
XLA Modules:
  0.0 138.7 jit_solution(5958425140087516566)
XLA Ops:
  0.0 1.0 copy.115
  1.8 6.1 %collective-permute-start.10 = (bf16[16,32,128]{2,1,0:T(8,128)(2,1)S(1)}, bf16[16,32,128]{2,1,0:T(8,128)(2,1)S(1)}, u32[]{:S(2)}, u32[]{:S(2)}) collective-permute-start(bf16[16,32,128]{2,1,0:T(8,128)(2,1)S(1)} %get-tuple-element.5), channel_id=1, source_target_pairs={{0,28},{1,29},{2,30},{3,31},{4,0},{5,1},{6,2},{7,3},{8,4},{9,5},{1... | collective-permute-start | bytes 393224 | tf_op jit(solution)/shard_map/ppermute | solution.py:15
  7.8 5.6 %collective-permute-start.6 = (bf16[16,32,128]{2,1,0:T(8,128)(2,1)S(1)}, bf16[16,32,128]{2,1,0:T(8,128)(2,1)S(1)}, u32[]{:S(2)}, u32[]{:S(2)}) collective-permute-start(bf16[16,32,128]{2,1,0:T(8,128)(2,1)S(1)} %get-tuple-element.5), channel_id=1, source_target_pairs={{0,30},{1,31},{2,0},{3,1},{4,2},{5,3},{6,4},{7,5},{8,6},{9,7},{10,... | collective-permute-start | bytes 393224 | tf_op jit(solution)/shard_map/ppermute | solution.py:15
  14.2 1.1 collective-permute-start.11
  17.8 8.3 %collective-permute-start.7 = (s32[8]{0:T(128)S(1)}, s32[8]{0:T(128)S(1)}, u32[]{:S(2)}, u32[]{:S(2)}) collective-permute-start(s32[8]{0:T(128)S(1)} %get-tuple-element.8), channel_id=1, source_target_pairs={{0,30},{1,31},{2,0},{3,1},{4,2},{5,3},{6,4},{7,5},{8,6},{9,7},{10,... | collective-permute-start | bytes 104 | tf_op jit(solution)/shard_map/ppermute | solution.py:15
  26.1 1.3 collective-permute-done.7
  27.4 7.3 %collective-permute-done.5 = s32[8]{0:T(128)S(1)} collective-permute-done((s32[8]{0:T(128)S(1)}, s32[8]{0:T(128)S(1)}, u32[]{:S(2)}, u32[]{:S(2)}) %collective-permute-start.5) | collective-permute-done | bytes 64 | tf_op jit(solution)/shard_map/ppermute | solution.py:15
  34.7 1.3 collective-permute-done.3
  36.1 6.5 %collective-permute-done.1 = s32[8]{0:T(128)S(1)} collective-permute-done((s32[8]{0:T(128)S(1)}, s32[8]{0:T(128)S(1)}, u32[]{:S(2)}, u32[]{:S(2)}) %collective-permute-start.1) | collective-permute-done | bytes 64 | tf_op jit(solution)/shard_map/ppermute | solution.py:15
  42.6 6.2 %collective-permute-done.9 = s32[8]{0:T(128)S(1)} collective-permute-done((s32[8]{0:T(128)S(1)}, s32[8]{0:T(128)S(1)}, u32[]{:S(2)}, u32[]{:S(2)}) %collective-permute-start.9) | collective-permute-done | bytes 64 | tf_op jit(solution)/shard_map/ppermute | solution.py:15
  52.6 4.3 %collective-permute-done = bf16[16,32,128]{2,1,0:T(8,128)(2,1)S(1)} collective-permute-done((bf16[16,32,128]{2,1,0:T(8,128)(2,1)S(1)}, bf16[16,32,128]{2,1,0:T(8,128)(2,1)S(1)}, u32[]{:S(2)}, u32[]{:S(2)}) %collective-permute-start) | collective-permute-done | bytes 131104 | tf_op jit(solution)/shard_map/ppermute | solution.py:15
  58.5 4.5 %fusion.24 = f32[128,16,128]{2,1,0:T(8,128)S(1)} fusion(bf16[128,128,128]{2,1,0:T(8,128)(2,1)} %param.6, bf16[128,16,128]{2,1,0:T(8,128)(2,1)S(1)} %gather_fusion.6), kind=kOutput, calls=%fused_computation.56 | convolution fusion | flops 67108864 | bytes 5767168 | tf_op jit(solution)/shard_map/ckj,kij->kci/dot_general | solution.py:45
  62.9 0.8 constant_dynamic-update-slice_fusion.13
  63.8 2.0 %collective-permute-start.16 = (bf16[16,32,128]{2,1,0:T(8,128)(2,1)S(1)}, bf16[16,32,128]{2,1,0:T(8,128)(2,1)S(1)}, u32[]{:S(2)}, u32[]{:S(2)}) collective-permute-start(bf16[16,32,128]{2,1,0:T(8,128)(2,1)S(1)} %get-tuple-element.14), channel_id=1, source_target_pairs={{0,4},{1,5},{2,6},{3,7},{4,8},{5,9},{6,10},{7,11},{8,12},{9,13},{1... | collective-permute-start | bytes 393224 | tf_op jit(solution)/shard_map/ppermute | solution.py:15
  65.8 2.0 %collective-permute-start.14 = (bf16[16,32,128]{2,1,0:T(8,128)(2,1)S(1)}, bf16[16,32,128]{2,1,0:T(8,128)(2,1)S(1)}, u32[]{:S(2)}, u32[]{:S(2)}) collective-permute-start(bf16[16,32,128]{2,1,0:T(8,128)(2,1)S(1)} %get-tuple-element.14), channel_id=1, source_target_pairs={{0,2},{1,3},{2,4},{3,5},{4,6},{5,7},{6,8},{7,9},{8,10},{9,11},{10,... | collective-permute-start | bytes 393224 | tf_op jit(solution)/shard_map/ppermute | solution.py:15
  67.8 5.8 %collective-permute-start.13 = (bf16[16,32,128]{2,1,0:T(8,128)(2,1)S(1)}, bf16[16,32,128]{2,1,0:T(8,128)(2,1)S(1)}, u32[]{:S(2)}, u32[]{:S(2)}) collective-permute-start(bf16[16,32,128]{2,1,0:T(8,128)(2,1)S(1)} %get-tuple-element.14), channel_id=1, source_target_pairs={{0,31},{1,0},{2,1},{3,2},{4,3},{5,4},{6,5},{7,6},{8,7},{9,8},{10,9... | collective-permute-start | bytes 393224 | tf_op jit(solution)/shard_map/ppermute | solution.py:15
  76.8 4.8 %collective-permute-done.12 = bf16[16,32,128]{2,1,0:T(8,128)(2,1)S(1)} collective-permute-done((bf16[16,32,128]{2,1,0:T(8,128)(2,1)S(1)}, bf16[16,32,128]{2,1,0:T(8,128)(2,1)S(1)}, u32[]{:S(2)}, u32[]{:S(2)}) %collective-permute-start.12) | collective-permute-done | bytes 131104 | tf_op jit(solution)/shard_map/ppermute | solution.py:15
  83.1 4.5 %fusion.22 = f32[128,16,128]{2,1,0:T(8,128)S(1)} fusion(bf16[128,128,128]{2,1,0:T(8,128)(2,1)} %param.6, bf16[128,16,128]{2,1,0:T(8,128)(2,1)S(1)} %gather_fusion.13), kind=kOutput, calls=%fused_computation.54 | convolution fusion | flops 67108864 | bytes 5767168 | tf_op jit(solution)/shard_map/ckj,kij->kci/dot_general | solution.py:45
  87.6 0.8 constant_dynamic-update-slice_fusion.20
  88.5 2.0 %collective-permute-start.22 = (bf16[16,32,128]{2,1,0:T(8,128)(2,1)S(1)}, bf16[16,32,128]{2,1,0:T(8,128)(2,1)S(1)}, u32[]{:S(2)}, u32[]{:S(2)}) collective-permute-start(bf16[16,32,128]{2,1,0:T(8,128)(2,1)S(1)} %get-tuple-element.16), channel_id=1, source_target_pairs={{0,4},{1,5},{2,6},{3,7},{4,8},{5,9},{6,10},{7,11},{8,12},{9,13},{1... | collective-permute-start | bytes 393224 | tf_op jit(solution)/shard_map/ppermute | solution.py:15
  90.5 2.0 %collective-permute-start.20 = (bf16[16,32,128]{2,1,0:T(8,128)(2,1)S(1)}, bf16[16,32,128]{2,1,0:T(8,128)(2,1)S(1)}, u32[]{:S(2)}, u32[]{:S(2)}) collective-permute-start(bf16[16,32,128]{2,1,0:T(8,128)(2,1)S(1)} %get-tuple-element.16), channel_id=1, source_target_pairs={{0,2},{1,3},{2,4},{3,5},{4,6},{5,7},{6,8},{7,9},{8,10},{9,11},{10,... | collective-permute-start | bytes 393224 | tf_op jit(solution)/shard_map/ppermute | solution.py:15
  92.5 5.8 %collective-permute-start.19 = (bf16[16,32,128]{2,1,0:T(8,128)(2,1)S(1)}, bf16[16,32,128]{2,1,0:T(8,128)(2,1)S(1)}, u32[]{:S(2)}, u32[]{:S(2)}) collective-permute-start(bf16[16,32,128]{2,1,0:T(8,128)(2,1)S(1)} %get-tuple-element.16), channel_id=1, source_target_pairs={{0,31},{1,0},{2,1},{3,2},{4,3},{5,4},{6,5},{7,6},{8,7},{9,8},{10,9... | collective-permute-start | bytes 393224 | tf_op jit(solution)/shard_map/ppermute | solution.py:15
  101.5 4.8 %collective-permute-done.18 = bf16[16,32,128]{2,1,0:T(8,128)(2,1)S(1)} collective-permute-done((bf16[16,32,128]{2,1,0:T(8,128)(2,1)S(1)}, bf16[16,32,128]{2,1,0:T(8,128)(2,1)S(1)}, u32[]{:S(2)}, u32[]{:S(2)}) %collective-permute-start.18) | collective-permute-done | bytes 131104 | tf_op jit(solution)/shard_map/ppermute | solution.py:15
  107.9 4.5 %fusion.20 = f32[128,16,128]{2,1,0:T(8,128)S(1)} fusion(bf16[128,128,128]{2,1,0:T(8,128)(2,1)} %param.6, bf16[128,16,128]{2,1,0:T(8,128)(2,1)S(1)} %gather_fusion.20), kind=kOutput, calls=%fused_computation.52 | convolution fusion | flops 67108864 | bytes 5767168 | tf_op jit(solution)/shard_map/ckj,kij->kci/dot_general | solution.py:45
  112.3 0.8 constant_dynamic-update-slice_fusion.27
  113.2 2.0 %collective-permute-start.28 = (bf16[16,32,128]{2,1,0:T(8,128)(2,1)S(1)}, bf16[16,32,128]{2,1,0:T(8,128)(2,1)S(1)}, u32[]{:S(2)}, u32[]{:S(2)}) collective-permute-start(bf16[16,32,128]{2,1,0:T(8,128)(2,1)S(1)} %get-tuple-element.18), channel_id=1, source_target_pairs={{0,4},{1,5},{2,6},{3,7},{4,8},{5,9},{6,10},{7,11},{8,12},{9,13},{1... | collective-permute-start | bytes 393224 | tf_op jit(solution)/shard_map/ppermute | solution.py:15
  115.2 2.0 %collective-permute-start.26 = (bf16[16,32,128]{2,1,0:T(8,128)(2,1)S(1)}, bf16[16,32,128]{2,1,0:T(8,128)(2,1)S(1)}, u32[]{:S(2)}, u32[]{:S(2)}) collective-permute-start(bf16[16,32,128]{2,1,0:T(8,128)(2,1)S(1)} %get-tuple-element.18), channel_id=1, source_target_pairs={{0,2},{1,3},{2,4},{3,5},{4,6},{5,7},{6,8},{7,9},{8,10},{9,11},{10,... | collective-permute-start | bytes 393224 | tf_op jit(solution)/shard_map/ppermute | solution.py:15
  117.2 5.8 %collective-permute-start.25 = (bf16[16,32,128]{2,1,0:T(8,128)(2,1)S(1)}, bf16[16,32,128]{2,1,0:T(8,128)(2,1)S(1)}, u32[]{:S(2)}, u32[]{:S(2)}) collective-permute-start(bf16[16,32,128]{2,1,0:T(8,128)(2,1)S(1)} %get-tuple-element.18), channel_id=1, source_target_pairs={{0,31},{1,0},{2,1},{3,2},{4,3},{5,4},{6,5},{7,6},{8,7},{9,8},{10,9... | collective-permute-start | bytes 393224 | tf_op jit(solution)/shard_map/ppermute | solution.py:15
  126.2 4.8 %collective-permute-done.24 = bf16[16,32,128]{2,1,0:T(8,128)(2,1)S(1)} collective-permute-done((bf16[16,32,128]{2,1,0:T(8,128)(2,1)S(1)}, bf16[16,32,128]{2,1,0:T(8,128)(2,1)S(1)}, u32[]{:S(2)}, u32[]{:S(2)}) %collective-permute-start.24) | collective-permute-done | bytes 131104 | tf_op jit(solution)/shard_map/ppermute | solution.py:15
  132.6 4.5 %fusion.18 = f32[128,16,128]{2,1,0:T(8,128)S(1)} fusion(bf16[128,128,128]{2,1,0:T(8,128)(2,1)} %param.6, bf16[128,16,128]{2,1,0:T(8,128)(2,1)S(1)} %gather_fusion.27), kind=kOutput, calls=%fused_computation.50 | convolution fusion | flops 67108864 | bytes 5767168 | tf_op jit(solution)/shard_map/ckj,kij->kci/dot_general | solution.py:45
  137.0 0.8 fusion.4
  137.8 0.9 copy.156
  (140 shorter events, 23.3 us)
Async XLA Ops:
  1.8 47.1 %collective-permute-start.10 = (bf16[16,32,128]{2,1,0:T(8,128)(2,1)S(1)}, bf16[16,32,128]{2,1,0:T(8,128)(2,1)S(1)}, u32[]{:S(2)}, u32[]{:S(2)}) collective-permute-start(bf16[16,32,128]{2,1,0:T(8,128)(2,1)S(1)} %get-tuple-element.5), channel_id=1, source_target_pairs={{0,28},{1,29},{2,30},{3,31},{4,0},{5,1},{6,2},{7,3},{8,4},{9,5},{1... | collective-permute-start | bytes 393224 | tf_op jit(solution)/shard_map/ppermute | solution.py:15
  7.8 42.2 %collective-permute-start.8 = (bf16[16,32,128]{2,1,0:T(8,128)(2,1)S(1)}, bf16[16,32,128]{2,1,0:T(8,128)(2,1)S(1)}, u32[]{:S(2)}, u32[]{:S(2)}) collective-permute-start(bf16[16,32,128]{2,1,0:T(8,128)(2,1)S(1)} %get-tuple-element.5), channel_id=1, source_target_pairs={{0,4},{1,5},{2,6},{3,7},{4,8},{5,9},{6,10},{7,11},{8,12},{9,13},{1... | collective-permute-start | bytes 393224 | tf_op jit(solution)/shard_map/ppermute | solution.py:15
  7.8 42.9 %collective-permute-start.6 = (bf16[16,32,128]{2,1,0:T(8,128)(2,1)S(1)}, bf16[16,32,128]{2,1,0:T(8,128)(2,1)S(1)}, u32[]{:S(2)}, u32[]{:S(2)}) collective-permute-start(bf16[16,32,128]{2,1,0:T(8,128)(2,1)S(1)} %get-tuple-element.5), channel_id=1, source_target_pairs={{0,30},{1,31},{2,0},{3,1},{4,2},{5,3},{6,4},{7,5},{8,6},{9,7},{10,... | collective-permute-start | bytes 393224 | tf_op jit(solution)/shard_map/ppermute | solution.py:15
  13.5 37.9 %collective-permute-start.4 = (bf16[16,32,128]{2,1,0:T(8,128)(2,1)S(1)}, bf16[16,32,128]{2,1,0:T(8,128)(2,1)S(1)}, u32[]{:S(2)}, u32[]{:S(2)}) collective-permute-start(bf16[16,32,128]{2,1,0:T(8,128)(2,1)S(1)} %get-tuple-element.5), channel_id=1, source_target_pairs={{0,2},{1,3},{2,4},{3,5},{4,6},{5,7},{6,8},{7,9},{8,10},{9,11},{10,... | collective-permute-start | bytes 393224 | tf_op jit(solution)/shard_map/ppermute | solution.py:15
  14.2 3.5 %collective-permute-start.11 = (s32[8]{0:T(128)S(1)}, s32[8]{0:T(128)S(1)}, u32[]{:S(2)}, u32[]{:S(2)}) collective-permute-start(s32[8]{0:T(128)S(1)} %get-tuple-element.7), channel_id=1, source_target_pairs={{0,28},{1,29},{2,30},{3,31},{4,0},{5,1},{6,2},{7,3},{8,4},{9,5},{1... | collective-permute-start | bytes 104 | tf_op jit(solution)/shard_map/ppermute | solution.py:15
  17.8 9.6 %collective-permute-start.7 = (s32[8]{0:T(128)S(1)}, s32[8]{0:T(128)S(1)}, u32[]{:S(2)}, u32[]{:S(2)}) collective-permute-start(s32[8]{0:T(128)S(1)} %get-tuple-element.8), channel_id=1, source_target_pairs={{0,30},{1,31},{2,0},{3,1},{4,2},{5,3},{6,4},{7,5},{8,6},{9,7},{10,... | collective-permute-start | bytes 104 | tf_op jit(solution)/shard_map/ppermute | solution.py:15
  27.4 7.4 %collective-permute-start.5 = (s32[8]{0:T(128)S(1)}, s32[8]{0:T(128)S(1)}, u32[]{:S(2)}, u32[]{:S(2)}) collective-permute-start(s32[8]{0:T(128)S(1)} %get-tuple-element.9), channel_id=1, source_target_pairs={{0,2},{1,3},{2,4},{3,5},{4,6},{5,7},{6,8},{7,9},{8,10},{9,11},{10,... | collective-permute-start | bytes 104 | tf_op jit(solution)/shard_map/ppermute | solution.py:15
  34.7 1.3 collective-permute-start.3
  36.0 6.6 %collective-permute-start.1 = (s32[8]{0:T(128)S(1)}, s32[8]{0:T(128)S(1)}, u32[]{:S(2)}, u32[]{:S(2)}) collective-permute-start(s32[8]{0:T(128)S(1)} %get-tuple-element.11), channel_id=1, source_target_pairs={{0,1},{1,2},{2,3},{3,4},{4,5},{5,6},{6,7},{7,8},{8,9},{9,10},{10,1... | collective-permute-start | bytes 104 | tf_op jit(solution)/shard_map/ppermute | solution.py:15
  42.6 6.2 %collective-permute-start.9 = (s32[8]{0:T(128)S(1)}, s32[8]{0:T(128)S(1)}, u32[]{:S(2)}, u32[]{:S(2)}) collective-permute-start(s32[8]{0:T(128)S(1)} %get-tuple-element.12), channel_id=1, source_target_pairs={{0,4},{1,5},{2,6},{3,7},{4,8},{5,9},{6,10},{7,11},{8,12},{9,13},{1... | collective-permute-start | bytes 104 | tf_op jit(solution)/shard_map/ppermute | solution.py:15
  48.8 3.2 %collective-permute-start.2 = (bf16[16,32,128]{2,1,0:T(8,128)(2,1)S(1)}, bf16[16,32,128]{2,1,0:T(8,128)(2,1)S(1)}, u32[]{:S(2)}, u32[]{:S(2)}) collective-permute-start(bf16[16,32,128]{2,1,0:T(8,128)(2,1)S(1)} %get-tuple-element.5), channel_id=1, source_target_pairs={{0,31},{1,0},{2,1},{3,2},{4,3},{5,4},{6,5},{7,6},{8,7},{9,8},{10,9... | collective-permute-start | bytes 393224 | tf_op jit(solution)/shard_map/ppermute | solution.py:15
  48.9 8.0 %collective-permute-start = (bf16[16,32,128]{2,1,0:T(8,128)(2,1)S(1)}, bf16[16,32,128]{2,1,0:T(8,128)(2,1)S(1)}, u32[]{:S(2)}, u32[]{:S(2)}) collective-permute-start(bf16[16,32,128]{2,1,0:T(8,128)(2,1)S(1)} %get-tuple-element.5), channel_id=1, source_target_pairs={{0,1},{1,2},{2,3},{3,4},{4,5},{5,6},{6,7},{7,8},{8,9},{9,10},{10,1... | collective-permute-start | bytes 393224 | tf_op jit(solution)/shard_map/ppermute | solution.py:15
  52.1 10.9 %copy-start = (f32[4096]{0:T(1024)S(1)}, f32[4096]{0:T(1024)}, u32[]{:S(2)}) copy-start(f32[4096]{0:T(1024)} %param.10) | copy-start | bytes 49156
  63.7 9.9 %collective-permute-start.17 = (bf16[16,32,128]{2,1,0:T(8,128)(2,1)S(1)}, bf16[16,32,128]{2,1,0:T(8,128)(2,1)S(1)}, u32[]{:S(2)}, u32[]{:S(2)}) collective-permute-start(bf16[16,32,128]{2,1,0:T(8,128)(2,1)S(1)} %get-tuple-element.14), channel_id=1, source_target_pairs={{0,28},{1,29},{2,30},{3,31},{4,0},{5,1},{6,2},{7,3},{8,4},{9,5},{1... | collective-permute-start | bytes 393224 | tf_op jit(solution)/shard_map/ppermute | solution.py:15
  63.8 10.4 %collective-permute-start.16 = (bf16[16,32,128]{2,1,0:T(8,128)(2,1)S(1)}, bf16[16,32,128]{2,1,0:T(8,128)(2,1)S(1)}, u32[]{:S(2)}, u32[]{:S(2)}) collective-permute-start(bf16[16,32,128]{2,1,0:T(8,128)(2,1)S(1)} %get-tuple-element.14), channel_id=1, source_target_pairs={{0,4},{1,5},{2,6},{3,7},{4,8},{5,9},{6,10},{7,11},{8,12},{9,13},{1... | collective-permute-start | bytes 393224 | tf_op jit(solution)/shard_map/ppermute | solution.py:15
  65.8 9.0 %collective-permute-start.15 = (bf16[16,32,128]{2,1,0:T(8,128)(2,1)S(1)}, bf16[16,32,128]{2,1,0:T(8,128)(2,1)S(1)}, u32[]{:S(2)}, u32[]{:S(2)}) collective-permute-start(bf16[16,32,128]{2,1,0:T(8,128)(2,1)S(1)} %get-tuple-element.14), channel_id=1, source_target_pairs={{0,30},{1,31},{2,0},{3,1},{4,2},{5,3},{6,4},{7,5},{8,6},{9,7},{10,... | collective-permute-start | bytes 393224 | tf_op jit(solution)/shard_map/ppermute | solution.py:15
  65.8 9.7 %collective-permute-start.14 = (bf16[16,32,128]{2,1,0:T(8,128)(2,1)S(1)}, bf16[16,32,128]{2,1,0:T(8,128)(2,1)S(1)}, u32[]{:S(2)}, u32[]{:S(2)}) collective-permute-start(bf16[16,32,128]{2,1,0:T(8,128)(2,1)S(1)} %get-tuple-element.14), channel_id=1, source_target_pairs={{0,2},{1,3},{2,4},{3,5},{4,6},{5,7},{6,8},{7,9},{8,10},{9,11},{10,... | collective-permute-start | bytes 393224 | tf_op jit(solution)/shard_map/ppermute | solution.py:15
  67.8 8.3 %collective-permute-start.13 = (bf16[16,32,128]{2,1,0:T(8,128)(2,1)S(1)}, bf16[16,32,128]{2,1,0:T(8,128)(2,1)S(1)}, u32[]{:S(2)}, u32[]{:S(2)}) collective-permute-start(bf16[16,32,128]{2,1,0:T(8,128)(2,1)S(1)} %get-tuple-element.14), channel_id=1, source_target_pairs={{0,31},{1,0},{2,1},{3,2},{4,3},{5,4},{6,5},{7,6},{8,7},{9,8},{10,9... | collective-permute-start | bytes 393224 | tf_op jit(solution)/shard_map/ppermute | solution.py:15
  73.6 8.0 %collective-permute-start.12 = (bf16[16,32,128]{2,1,0:T(8,128)(2,1)S(1)}, bf16[16,32,128]{2,1,0:T(8,128)(2,1)S(1)}, u32[]{:S(2)}, u32[]{:S(2)}) collective-permute-start(bf16[16,32,128]{2,1,0:T(8,128)(2,1)S(1)} %get-tuple-element.14), channel_id=1, source_target_pairs={{0,1},{1,2},{2,3},{3,4},{4,5},{5,6},{6,7},{7,8},{8,9},{9,10},{10,1... | collective-permute-start | bytes 393224 | tf_op jit(solution)/shard_map/ppermute | solution.py:15
  88.4 9.9 %collective-permute-start.23 = (bf16[16,32,128]{2,1,0:T(8,128)(2,1)S(1)}, bf16[16,32,128]{2,1,0:T(8,128)(2,1)S(1)}, u32[]{:S(2)}, u32[]{:S(2)}) collective-permute-start(bf16[16,32,128]{2,1,0:T(8,128)(2,1)S(1)} %get-tuple-element.16), channel_id=1, source_target_pairs={{0,28},{1,29},{2,30},{3,31},{4,0},{5,1},{6,2},{7,3},{8,4},{9,5},{1... | collective-permute-start | bytes 393224 | tf_op jit(solution)/shard_map/ppermute | solution.py:15
  88.5 10.5 %collective-permute-start.22 = (bf16[16,32,128]{2,1,0:T(8,128)(2,1)S(1)}, bf16[16,32,128]{2,1,0:T(8,128)(2,1)S(1)}, u32[]{:S(2)}, u32[]{:S(2)}) collective-permute-start(bf16[16,32,128]{2,1,0:T(8,128)(2,1)S(1)} %get-tuple-element.16), channel_id=1, source_target_pairs={{0,4},{1,5},{2,6},{3,7},{4,8},{5,9},{6,10},{7,11},{8,12},{9,13},{1... | collective-permute-start | bytes 393224 | tf_op jit(solution)/shard_map/ppermute | solution.py:15
  90.5 9.1 %collective-permute-start.21 = (bf16[16,32,128]{2,1,0:T(8,128)(2,1)S(1)}, bf16[16,32,128]{2,1,0:T(8,128)(2,1)S(1)}, u32[]{:S(2)}, u32[]{:S(2)}) collective-permute-start(bf16[16,32,128]{2,1,0:T(8,128)(2,1)S(1)} %get-tuple-element.16), channel_id=1, source_target_pairs={{0,30},{1,31},{2,0},{3,1},{4,2},{5,3},{6,4},{7,5},{8,6},{9,7},{10,... | collective-permute-start | bytes 393224 | tf_op jit(solution)/shard_map/ppermute | solution.py:15
  90.5 9.7 %collective-permute-start.20 = (bf16[16,32,128]{2,1,0:T(8,128)(2,1)S(1)}, bf16[16,32,128]{2,1,0:T(8,128)(2,1)S(1)}, u32[]{:S(2)}, u32[]{:S(2)}) collective-permute-start(bf16[16,32,128]{2,1,0:T(8,128)(2,1)S(1)} %get-tuple-element.16), channel_id=1, source_target_pairs={{0,2},{1,3},{2,4},{3,5},{4,6},{5,7},{6,8},{7,9},{8,10},{9,11},{10,... | collective-permute-start | bytes 393224 | tf_op jit(solution)/shard_map/ppermute | solution.py:15
  92.5 8.4 %collective-permute-start.19 = (bf16[16,32,128]{2,1,0:T(8,128)(2,1)S(1)}, bf16[16,32,128]{2,1,0:T(8,128)(2,1)S(1)}, u32[]{:S(2)}, u32[]{:S(2)}) collective-permute-start(bf16[16,32,128]{2,1,0:T(8,128)(2,1)S(1)} %get-tuple-element.16), channel_id=1, source_target_pairs={{0,31},{1,0},{2,1},{3,2},{4,3},{5,4},{6,5},{7,6},{8,7},{9,8},{10,9... | collective-permute-start | bytes 393224 | tf_op jit(solution)/shard_map/ppermute | solution.py:15
  98.3 8.0 %collective-permute-start.18 = (bf16[16,32,128]{2,1,0:T(8,128)(2,1)S(1)}, bf16[16,32,128]{2,1,0:T(8,128)(2,1)S(1)}, u32[]{:S(2)}, u32[]{:S(2)}) collective-permute-start(bf16[16,32,128]{2,1,0:T(8,128)(2,1)S(1)} %get-tuple-element.16), channel_id=1, source_target_pairs={{0,1},{1,2},{2,3},{3,4},{4,5},{5,6},{6,7},{7,8},{8,9},{9,10},{10,1... | collective-permute-start | bytes 393224 | tf_op jit(solution)/shard_map/ppermute | solution.py:15
  113.1 9.9 %collective-permute-start.29 = (bf16[16,32,128]{2,1,0:T(8,128)(2,1)S(1)}, bf16[16,32,128]{2,1,0:T(8,128)(2,1)S(1)}, u32[]{:S(2)}, u32[]{:S(2)}) collective-permute-start(bf16[16,32,128]{2,1,0:T(8,128)(2,1)S(1)} %get-tuple-element.18), channel_id=1, source_target_pairs={{0,28},{1,29},{2,30},{3,31},{4,0},{5,1},{6,2},{7,3},{8,4},{9,5},{1... | collective-permute-start | bytes 393224 | tf_op jit(solution)/shard_map/ppermute | solution.py:15
  113.2 10.5 %collective-permute-start.28 = (bf16[16,32,128]{2,1,0:T(8,128)(2,1)S(1)}, bf16[16,32,128]{2,1,0:T(8,128)(2,1)S(1)}, u32[]{:S(2)}, u32[]{:S(2)}) collective-permute-start(bf16[16,32,128]{2,1,0:T(8,128)(2,1)S(1)} %get-tuple-element.18), channel_id=1, source_target_pairs={{0,4},{1,5},{2,6},{3,7},{4,8},{5,9},{6,10},{7,11},{8,12},{9,13},{1... | collective-permute-start | bytes 393224 | tf_op jit(solution)/shard_map/ppermute | solution.py:15
  115.2 9.1 %collective-permute-start.27 = (bf16[16,32,128]{2,1,0:T(8,128)(2,1)S(1)}, bf16[16,32,128]{2,1,0:T(8,128)(2,1)S(1)}, u32[]{:S(2)}, u32[]{:S(2)}) collective-permute-start(bf16[16,32,128]{2,1,0:T(8,128)(2,1)S(1)} %get-tuple-element.18), channel_id=1, source_target_pairs={{0,30},{1,31},{2,0},{3,1},{4,2},{5,3},{6,4},{7,5},{8,6},{9,7},{10,... | collective-permute-start | bytes 393224 | tf_op jit(solution)/shard_map/ppermute | solution.py:15
  115.2 9.7 %collective-permute-start.26 = (bf16[16,32,128]{2,1,0:T(8,128)(2,1)S(1)}, bf16[16,32,128]{2,1,0:T(8,128)(2,1)S(1)}, u32[]{:S(2)}, u32[]{:S(2)}) collective-permute-start(bf16[16,32,128]{2,1,0:T(8,128)(2,1)S(1)} %get-tuple-element.18), channel_id=1, source_target_pairs={{0,2},{1,3},{2,4},{3,5},{4,6},{5,7},{6,8},{7,9},{8,10},{9,11},{10,... | collective-permute-start | bytes 393224 | tf_op jit(solution)/shard_map/ppermute | solution.py:15
  117.2 8.4 %collective-permute-start.25 = (bf16[16,32,128]{2,1,0:T(8,128)(2,1)S(1)}, bf16[16,32,128]{2,1,0:T(8,128)(2,1)S(1)}, u32[]{:S(2)}, u32[]{:S(2)}) collective-permute-start(bf16[16,32,128]{2,1,0:T(8,128)(2,1)S(1)} %get-tuple-element.18), channel_id=1, source_target_pairs={{0,31},{1,0},{2,1},{3,2},{4,3},{5,4},{6,5},{7,6},{8,7},{9,8},{10,9... | collective-permute-start | bytes 393224 | tf_op jit(solution)/shard_map/ppermute | solution.py:15
  123.0 8.0 %collective-permute-start.24 = (bf16[16,32,128]{2,1,0:T(8,128)(2,1)S(1)}, bf16[16,32,128]{2,1,0:T(8,128)(2,1)S(1)}, u32[]{:S(2)}, u32[]{:S(2)}) collective-permute-start(bf16[16,32,128]{2,1,0:T(8,128)(2,1)S(1)} %get-tuple-element.18), channel_id=1, source_target_pairs={{0,1},{1,2},{2,3},{3,4},{4,5},{5,6},{6,7},{7,8},{8,9},{9,10},{10,1... | collective-permute-start | bytes 393224 | tf_op jit(solution)/shard_map/ppermute | solution.py:15
where the time goes:
time: 139 us
  starting transfers between devices  51.4 us (37%)
  waiting for transfers between devices  41.7 us (30%)
  local copies, waits for them, and re-layouts  21.8 us (16%)
  matrix products  20.9 us (15%)
  other arithmetic  2.3 us (2%)
    ppermute x30, starting transfers between devices, passed_along(): return lax.ppermute(x, axis, [(i, (i + by) % count) for i in range(count)])  51.4 us
    ppermute x30, waiting for transfers between devices, passed_along(): return lax.ppermute(x, axis, [(i, (i + by) % count) for i in range(count)])  41.7 us
    dot_general x4, matrix products, on_device(): jnp.einsum('ckj,kij->kci', picked, blocks, preferred_element_type=jnp.flo...  17.8 us
    gather x24, local copies, waits for them, and re-layouts, on_device(): pieces.append(passed_along(scaled, 'dom', OFFSETS[j])[:, theirs[j]])  13.5 us
    dot_general x4, matrix products, on_device(): jnp.einsum('rk,kci->cri', onehot, prods, precision=lax.Precision.HIGHEST)  3.11 us
    gather x4, local copies, waits for them, and re-layouts, on_device(): picked = extended[:, columns]  2.82 us
  transfers between devices with their start and end apart: 30, of which 10 were waited for; matrix products, arithmetic and copies ran while one was open for 11% of the time, Pallas kernels for 0%

commit v1 on v0

v1 whole, which is shorter than its diff:
```python
import functools

import jax
import jax.numpy as jnp
from jax import lax
from jax.experimental import pallas as pl
from jax.experimental.pallas import tpu as pltpu
from jax.sharding import PartitionSpec as P

ITERS = 4
MAXR = 4
OFFSETS = (1, -1, 2, -2, 4, -4)
ORDER = (4, 5, 2, 3, 0, 1)
ALPHA = 0.8
CHUNKS = 4


def dot_nt(a, b):
    return lax.dot_general(a, b, (((1,), (1,)), ((), ())), preferred_element_type=jnp.float32)


def kernel(n, col_ref, off_ref, lists_ref, scale_ref, seeds_ref, blocks_ref, out_ref,
           w_ref, own_ref, acc_ref, ext_refs, send_refs, w_sem, send_sem, recv_sem):
    nnz, blk = w_ref.shape[0], w_ref.shape[1]
    nrb, width = own_ref.shape[0], own_ref.shape[1]
    parts, per = lists_ref.shape[1], lists_ref.shape[2]
    none = nrb + parts * per
    me = lax.axis_index("dom")
    partners = [lax.rem(me + (o + n), n) for o in OFFSETS]

    barrier = pltpu.get_barrier_semaphore()
    for p in partners:
        pl.semaphore_signal(barrier, inc=1, device_id=(p,), device_id_type=pl.DeviceIdType.MESH)

    span = nnz // CHUNKS
    loads = []
    for c in range(CHUNKS):
        load = pltpu.make_async_copy(
            blocks_ref.at[pl.ds(c * span, span)], w_ref.at[pl.ds(c * span, span)], w_sem.at[c])
        load.start()
        loads.append(load)

    for r in range(nrb):
        cols = pl.ds(r * blk, blk)
        scaled = (seeds_ref[:, cols] * scale_ref[r:r + 1, :]).astype(jnp.bfloat16)
        own_ref[r] = scaled
        ext_refs[0][r] = scaled
    for ext in ext_refs:
        ext[none] = jnp.zeros((width, blk), jnp.bfloat16)

    pl.semaphore_wait(barrier, parts)

    copies = []
    for step in range(ITERS):
        ext, send = ext_refs[step], send_refs[step]
        flying = []
        for j in ORDER:
            for h in range(per):
                send[j * per + h] = own_ref[lists_ref[0, j, h]]
            copy = pltpu.make_async_remote_copy(
                src_ref=send.at[pl.ds(j * per, per)],
                dst_ref=ext.at[pl.ds(nrb + j * per, per)],
                send_sem=send_sem.at[step, j],
                recv_sem=recv_sem.at[step, j],
                device_id=(partners[j],),
                device_id_type=pl.DeviceIdType.MESH,
            )
            copy.start()
            flying.append(copy)
        copies += flying

        if step == 0:
            for load in loads:
                load.wait()

        def first(r, carry):
            acc_ref[r] = dot_nt(ext[r], w_ref[off_ref[0, r]])
            return carry

        lax.fori_loop(0, nrb, first, 0, unroll=8)

        for copy in flying:
            copy.wait_recv()

        def rest(r, carry):
            begin, end = off_ref[0, r], off_ref[0, r + 1]
            xs, ws = [], []
            for k in range(1, MAXR):
                slot = jnp.minimum(begin + k, nnz - 1)
                col = jnp.where(begin + k < end, col_ref[0, slot], none)
                xs.append(ext[col])
                ws.append(w_ref[slot])
            total = acc_ref[r] + dot_nt(jnp.concatenate(xs, axis=1), jnp.concatenate(ws, axis=1))
            cols = pl.ds(pl.multiple_of(r * blk, blk), blk)
            scale = scale_ref[pl.ds(r, 1), :]
            field = ALPHA * scale * total + (1.0 - ALPHA) * seeds_ref[:, cols]
            if step == ITERS - 1:
                out_ref[:, cols] = field
            else:
                scaled = (field * scale).astype(jnp.bfloat16)
                own_ref[r] = scaled
                ext_refs[step + 1][r] = scaled
            return carry

        lax.fori_loop(0, nrb, rest, 0, unroll=8)

    for copy in copies:
        copy.wait_send()


def on_device(blocks, col_index, row_offsets, send_index, deg_scale, seeds):
    nnz, blk = blocks.shape[0], blocks.shape[1]
    width = seeds.shape[0]
    nrb = deg_scale.shape[0] // blk
    parts, per = send_index.shape[1], send_index.shape[2]
    n = lax.axis_size("dom")
    smem = pl.BlockSpec(memory_space=pltpu.SMEM)
    vmem = pl.BlockSpec(memory_space=pltpu.VMEM)
    return pl.pallas_call(
        functools.partial(kernel, n),
        out_shape=jax.ShapeDtypeStruct(seeds.shape, jnp.float32),
        in_specs=[smem, smem, smem, vmem, vmem, pl.BlockSpec(memory_space=pl.ANY)],
        out_specs=vmem,
        scratch_shapes=[
            pltpu.VMEM((nnz, blk, blk), jnp.bfloat16),
            pltpu.VMEM((nrb, width, blk), jnp.bfloat16),
            pltpu.VMEM((nrb, width, blk), jnp.float32),
            [pltpu.VMEM((nrb + parts * per + 1, width, blk), jnp.bfloat16) for _ in range(ITERS)],
            [pltpu.VMEM((parts * per, width, blk), jnp.bfloat16) for _ in range(ITERS)],
            pltpu.SemaphoreType.DMA((CHUNKS,)),
            pltpu.SemaphoreType.DMA((ITERS, parts)),
            pltpu.SemaphoreType.DMA((ITERS, parts)),
        ],
        compiler_params=pltpu.CompilerParams(
            collective_id=0, has_side_effects=True, vmem_limit_bytes=32 * 1024 * 1024),
        cost_estimate=pl.CostEstimate(
            flops=2 * ITERS * nnz * blk * blk * width,
            bytes_accessed=nnz * blk * blk * 2 + 3 * width * nrb * blk * 4,
            transcendentals=0),
        name="spread_all",
    )(col_index, row_offsets, send_index, deg_scale.reshape(nrb, blk), seeds, blocks)


def solution(mesh):
    in_specs = (
        P("dom", None, None),
        P("dom", None),
        P("dom", None),
        P("dom", None, None),
        P("dom"),
        P(None, "dom"),
    )
    out_specs = P(None, "dom")
    return jax.shard_map(
        on_device, mesh=mesh, in_specs=in_specs, out_specs=out_specs, check_vma=False
    )
```

time: 139 us -> 42.7 us (0.31)
  starting transfers between devices: 51.4 us -> 0 us
  waiting for transfers between devices: 41.7 us -> 0 us
  Pallas kernels: 0 us -> 35.8 us
  matrix products: 20.9 us -> 0 us
  local copies, waits for them, and re-layouts: 21.8 us -> 6.55 us
  other arithmetic: 2.3 us -> 0 us
    ppermute x30 -> x0, starting transfers between devices: 51.4 us -> none  [passed_along(): return lax.ppermute(x, axis, [(i, (i + by) % count) for i in range(count)])]
    ppermute x30 -> x0, waiting for transfers between devices: 41.7 us -> none  [passed_along(): return lax.ppermute(x, axis, [(i, (i + by) % count) for i in range(count)])]
    pallas_call x0 -> x1, Pallas kernels: none -> 35.8 us  [on_device(): pl.pallas_call(functools.partial(kernel, n), out_shape=jax.ShapeDtypeStru...]
    dot_general x8 -> x0, matrix products: 20.9 us -> none  [the longest x4 17.8 us: on_device(): jnp.einsum('ckj,kij->kci', picked, blocks, preferred_element_type=jnp.flo...]
    gather x28 -> x0, local copies, waits for them, and re-layouts: 16.3 us -> none  [the longest x24 13.5 us: on_device(): pieces.append(passed_along(scaled, 'dom', OFFSETS[j])[:, theirs[j]])]
    unnamed x25 -> x12, local copies, waits for them, and re-layouts: 2.24 us -> 6.55 us
  transfers between devices with their start and end apart: 30 -> 0, of which waited for: 10 -> 0; matrix products, arithmetic and copies ran while one was open for 11% -> 0% of each run, Pallas kernels for 0% -> 0%
where the time goes in v1:
time: 42.7 us; the launch traced here: 42.4 us
  Pallas kernels  35.8 us (84%)
  local copies, waits for them, and re-layouts  6.55 us (15%)
    pallas_call x1, Pallas kernels, on_device(): pl.pallas_call(functools.partial(kernel, n), out_shape=jax.ShapeDtypeStru...  35.8 us
    unnamed x12, local copies, waits for them, and re-layouts  6.55 us

profile of v1, /device:TPU:0, one launch (start us, length us, event | category | flops | bytes accessed | tf_op | source)
XLA Modules:
  0.0 42.4 jit_solution(14242217232366280186)
XLA Ops:
  0.0 0.7 %copy.7.lists_ref = s32[1,6,8]{2,1,0:T(8,128)S(1)} copy(s32[1,6,8]{2,0,1:T(1,128)} %param.9) | data formatting | bytes 384 | tf_op args[3]
  0.7 0.0 copy-start
  0.7 2.2 %copy-done = bf16[128,128,128]{2,1,0:T(8,128)(2,1)S(1)} copy-done((bf16[128,128,128]{2,1,0:T(8,128)(2,1)S(1)}, bf16[128,128,128]{2,1,0:T(8,128)(2,1)}, u32[]{:S(2)}) %copy-start) | copy-done | bytes 4194328
  2.9 0.0 copy-start.1
  2.9 0.9 %copy-done.1 = f32[16,4096]{1,0:T(8,128)S(1)} copy-done((f32[16,4096]{1,0:T(8,128)S(1)}, f32[16,4096]{1,0:T(8,128)}, u32[]{:S(2)}) %copy-start.1) | copy-done | bytes 262168
  3.8 0.0 copy-start.2
  3.8 0.7 %copy-done.2 = f32[4096]{0:T(1024)S(1)} copy-done((f32[4096]{0:T(1024)S(1)}, f32[4096]{0:T(1024)}, u32[]{:S(2)}) %copy-start.2) | copy-done | bytes 16408
  4.5 0.0 copy-start.3
  4.5 0.7 %copy-done.3 = s32[1,128]{1,0:T(1,128)S(1)} copy-done((s32[1,128]{1,0:T(1,128)S(1)}, s32[1,128]{1,0:T(1,128)}, u32[]{:S(2)}) %copy-start.3) | copy-done | bytes 536
  5.2 0.0 copy-start.4
  5.2 0.7 %copy-done.4 = s32[1,33]{1,0:T(1,128)S(1)} copy-done((s32[1,33]{1,0:T(1,128)S(1)}, s32[1,33]{1,0:T(1,128)}, u32[]{:S(2)}) %copy-start.4) | copy-done | bytes 156
  5.9 35.8 %spread_all.1 = f32[16,4096]{1,0:T(8,128)S(1)} custom-call(s32[1,128]{1,0:T(1,128)S(1)} %copy-done.3, s32[1,33]{1,0:T(1,128)S(1)} %copy-done.4, s32[1,6,8]{2,1,0:T(8,128)S(1)} %copy.7.lists_ref, f32[32,128]{1,0:T(8,128)S(1)} %bitcast.1, f32[16,4096]{1,0:T(8,128)S(1)} %copy-done.1, bf16[128,128,128]{2,1,0:T(8,128)(2,1)S(1)} %copy-done), custom_call_target="tpu_custom_call" | custom-call | flops 268435456 | bytes 4980736 | tf_op jit(solution)/shard_map/spread_all/pallas_call | solution.py:119
  41.7 0.7 %copy.9 = f32[16,4096]{1,0:T(8,128)} copy(f32[16,4096]{1,0:T(8,128)S(1)} %spread_all.1) | data formatting | bytes 524288
Async XLA Ops:
  0.7 2.2 %copy-start = (bf16[128,128,128]{2,1,0:T(8,128)(2,1)S(1)}, bf16[128,128,128]{2,1,0:T(8,128)(2,1)}, u32[]{:S(2)}) copy-start(bf16[128,128,128]{2,1,0:T(8,128)(2,1)} %blocks_ref.1) | copy-start | bytes 12582916
  2.9 0.9 %copy-start.1 = (f32[16,4096]{1,0:T(8,128)S(1)}, f32[16,4096]{1,0:T(8,128)}, u32[]{:S(2)}) copy-start(f32[16,4096]{1,0:T(8,128)} %seeds_ref.1) | copy-start | bytes 786436
  3.8 0.7 %copy-start.2 = (f32[4096]{0:T(1024)S(1)}, f32[4096]{0:T(1024)}, u32[]{:S(2)}) copy-start(f32[4096]{0:T(1024)} %param.10) | copy-start | bytes 49156
  4.5 0.7 %copy-start.3 = (s32[1,128]{1,0:T(1,128)S(1)}, s32[1,128]{1,0:T(1,128)}, u32[]{:S(2)}) copy-start(s32[1,128]{1,0:T(1,128)} %col_ref.1) | copy-start | bytes 1540
  5.2 0.7 %copy-start.4 = (s32[1,33]{1,0:T(1,128)S(1)}, s32[1,33]{1,0:T(1,128)}, u32[]{:S(2)}) copy-start(s32[1,33]{1,0:T(1,128)} %off_ref.1) | copy-start | bytes 400

commit v2 on v1

--- a/solution.py
+++ b/solution.py
@@ -19,11 +19,12 @@
     return lax.dot_general(a, b, (((1,), (1,)), ((), ())), preferred_element_type=jnp.float32)
 
 
-def kernel(n, col_ref, off_ref, lists_ref, scale_ref, seeds_ref, blocks_ref, out_ref,
-           w_ref, own_ref, acc_ref, ext_refs, send_refs, w_sem, send_sem, recv_sem):
+def kernel(n, col_hbm, off_hbm, lists_hbm, scale_hbm, seeds_hbm, blocks_ref, out_ref,
+           col_ref, off_ref, lists_ref, scale_ref, seeds_ref,
+           w_ref, own_ref, acc_ref, ext_refs, send_refs, in_sem, w_sem, send_sem, recv_sem):
     nnz, blk = w_ref.shape[0], w_ref.shape[1]
     nrb, width = own_ref.shape[0], own_ref.shape[1]
-    parts, per = lists_ref.shape[1], lists_ref.shape[2]
+    parts, per = lists_ref.shape[0], lists_ref.shape[2]
     none = nrb + parts * per
     me = lax.axis_index("dom")
     partners = [lax.rem(me + (o + n), n) for o in OFFSETS]
@@ -32,6 +33,13 @@
     for p in partners:
         pl.semaphore_signal(barrier, inc=1, device_id=(p,), device_id_type=pl.DeviceIdType.MESH)
 
+    small = []
+    pairs = ((seeds_hbm, seeds_ref), (scale_hbm, scale_ref), (lists_hbm, lists_ref),
+             (off_hbm, off_ref), (col_hbm, col_ref))
+    for i, (src, dst) in enumerate(pairs):
+        load = pltpu.make_async_copy(src, dst, in_sem.at[i])
+        load.start()
+        small.append(load)
     span = nnz // CHUNKS
     loads = []
     for c in range(CHUNKS):
@@ -40,13 +48,16 @@
         load.start()
         loads.append(load)
 
+    for ext in ext_refs:
+        ext[none] = jnp.zeros((width, blk), jnp.bfloat16)
+    for load in small:
+        load.wait()
+
     for r in range(nrb):
         cols = pl.ds(r * blk, blk)
         scaled = (seeds_ref[:, cols] * scale_ref[r:r + 1, :]).astype(jnp.bfloat16)
         own_ref[r] = scaled
         ext_refs[0][r] = scaled
-    for ext in ext_refs:
-        ext[none] = jnp.zeros((width, blk), jnp.bfloat16)
 
     pl.semaphore_wait(barrier, parts)
 
@@ -56,7 +67,7 @@
         flying = []
         for j in ORDER:
             for h in range(per):
-                send[j * per + h] = own_ref[lists_ref[0, j, h]]
+                send[j * per + h] = own_ref[lists_ref[j, 0, h]]
             copy = pltpu.make_async_remote_copy(
                 src_ref=send.at[pl.ds(j * per, per)],
                 dst_ref=ext.at[pl.ds(nrb + j * per, per)],
@@ -114,31 +125,36 @@
     nrb = deg_scale.shape[0] // blk
     parts, per = send_index.shape[1], send_index.shape[2]
     n = lax.axis_size("dom")
-    smem = pl.BlockSpec(memory_space=pltpu.SMEM)
-    vmem = pl.BlockSpec(memory_space=pltpu.VMEM)
+    hbm = pl.BlockSpec(memory_space=pltpu.HBM)
     return pl.pallas_call(
         functools.partial(kernel, n),
         out_shape=jax.ShapeDtypeStruct(seeds.shape, jnp.float32),
-        in_specs=[smem, smem, smem, vmem, vmem, pl.BlockSpec(memory_space=pl.ANY)],
-        out_specs=vmem,
+        in_specs=[hbm] * 6,
+        out_specs=pl.BlockSpec(memory_space=pltpu.VMEM),
         scratch_shapes=[
+            pltpu.SMEM(col_index.shape, jnp.int32),
+            pltpu.SMEM(row_offsets.shape, jnp.int32),
+            pltpu.SMEM((parts, 1, per), jnp.int32),
+            pltpu.VMEM((nrb, blk), jnp.float32),
+            pltpu.VMEM(seeds.shape, jnp.float32),
             pltpu.VMEM((nnz, blk, blk), jnp.bfloat16),
             pltpu.VMEM((nrb, width, blk), jnp.bfloat16),
             pltpu.VMEM((nrb, width, blk), jnp.float32),
             [pltpu.VMEM((nrb + parts * per + 1, width, blk), jnp.bfloat16) for _ in range(ITERS)],
             [pltpu.VMEM((parts * per, width, blk), jnp.bfloat16) for _ in range(ITERS)],
+            pltpu.SemaphoreType.DMA((5,)),
             pltpu.SemaphoreType.DMA((CHUNKS,)),
             pltpu.SemaphoreType.DMA((ITERS, parts)),
             pltpu.SemaphoreType.DMA((ITERS, parts)),
         ],
         compiler_params=pltpu.CompilerParams(
-            collective_id=0, has_side_effects=True, vmem_limit_bytes=32 * 1024 * 1024),
+            collective_id=0, has_side_effects=True, vmem_limit_bytes=64 * 1024 * 1024),
         cost_estimate=pl.CostEstimate(
             flops=2 * ITERS * nnz * blk * blk * width,
             bytes_accessed=nnz * blk * blk * 2 + 3 * width * nrb * blk * 4,
             transcendentals=0),
         name="spread_all",
-    )(col_index, row_offsets, send_index, deg_scale.reshape(nrb, blk), seeds, blocks)
+    )(col_index, row_offsets, send_index.transpose(1, 0, 2), deg_scale.reshape(nrb, blk), seeds, blocks)
 
 
 def solution(mesh):

time: 42.7 us -> 37.7 us (0.88)
  local copies, waits for them, and re-layouts: 6.55 us -> 1.67 us
    unnamed x12 -> x1, local copies, waits for them, and re-layouts: 6.55 us -> 1.67 us
where the time goes in v2:
time: 37.7 us; the launch traced here: 37.6 us
  Pallas kernels  35.9 us (95%)
  local copies, waits for them, and re-layouts  1.67 us (4%)
    pallas_call x1, Pallas kernels, on_device(): pl.pallas_call(functools.partial(kernel, n), out_shape=jax.ShapeDtypeStru...  35.9 us
    unnamed x1, local copies, waits for them, and re-layouts  1.67 us

profile of v2, /device:TPU:0, one launch (start us, length us, event | category | flops | bytes accessed | tf_op | source)
XLA Modules:
  0.0 37.6 jit_solution(7287457452201336258)
XLA Ops:
  0.0 35.9 %spread_all.1 = f32[16,4096]{1,0:T(8,128)} custom-call(s32[1,128]{1,0:T(1,128)} %col_hbm.1, s32[1,33]{1,0:T(1,128)} %off_hbm.1, s32[6,1,8]{2,1,0:T(1,128)} %bitcast.3, f32[32,128]{1,0:T(8,128)} %bitcast.2, f32[16,4096]{1,0:T(8,128)} %seeds_hbm.1, bf16[128,128,128]{2,1,0:T(8,128)(2,1)} %blocks_ref.1), custom_call_target="tpu_custom_call" | custom-call | flops 268435456 | bytes 4980736 | tf_op jit(solution)/shard_map/spread_all/pallas_call | solution.py:129
  35.9 1.7 %copy.8 = f32[16,4096]{1,0:T(8,128)} copy(f32[16,4096]{1,0:T(8,128)} %spread_all.1) | data formatting | bytes 524288

commit v3 on v2

--- a/solution.py
+++ b/solution.py
@@ -15,8 +15,9 @@
 CHUNKS = 4
 
 
-def dot_nt(a, b):
-    return lax.dot_general(a, b, (((1,), (1,)), ((), ())), preferred_element_type=jnp.float32)
+def dot_nt(x, w):
+    turned = lax.dot_general(w, x, (((1,), (1,)), ((), ())), preferred_element_type=jnp.float32)
+    return turned.T
 
 
 def kernel(n, col_hbm, off_hbm, lists_hbm, scale_hbm, seeds_hbm, blocks_ref, out_ref,
@@ -88,7 +89,7 @@
             acc_ref[r] = dot_nt(ext[r], w_ref[off_ref[0, r]])
             return carry
 
-        lax.fori_loop(0, nrb, first, 0, unroll=8)
+        lax.fori_loop(0, nrb, first, 0, unroll=True)
 
         for copy in flying:
             copy.wait_recv()
@@ -113,7 +114,7 @@
                 ext_refs[step + 1][r] = scaled
             return carry
 
-        lax.fori_loop(0, nrb, rest, 0, unroll=8)
+        lax.fori_loop(0, nrb, rest, 0, unroll=True)
 
     for copy in copies:
         copy.wait_send()

time: 37.7 us -> 35.7 us (0.947)
  Pallas kernels: 35.9 us -> 33.9 us
    pallas_call x1, Pallas kernels: 35.9 us -> 33.9 us  [on_device(): pl.pallas_call(functools.partial(kernel, n), out_shape=jax.ShapeDtypeStru...]
where the time goes in v3:
time: 35.7 us; the launch traced here: 35.5 us
  Pallas kernels  33.9 us (95%)
  local copies, waits for them, and re-layouts  1.67 us (5%)
    pallas_call x1, Pallas kernels, on_device(): pl.pallas_call(functools.partial(kernel, n), out_shape=jax.ShapeDtypeStru...  33.9 us
    unnamed x1, local copies, waits for them, and re-layouts  1.67 us

profile of v3, /device:TPU:0, one launch (start us, length us, event | category | flops | bytes accessed | tf_op | source)
XLA Modules:
  0.0 35.5 jit_solution(703028568162619370)
XLA Ops:
  0.0 33.9 %spread_all.1 = f32[16,4096]{1,0:T(8,128)} custom-call(s32[1,128]{1,0:T(1,128)} %col_hbm.1, s32[1,33]{1,0:T(1,128)} %off_hbm.1, s32[6,1,8]{2,1,0:T(1,128)} %bitcast.3, f32[32,128]{1,0:T(8,128)} %bitcast.2, f32[16,4096]{1,0:T(8,128)} %seeds_hbm.1, bf16[128,128,128]{2,1,0:T(8,128)(2,1)} %blocks_ref.1), custom_call_target="tpu_custom_call" | custom-call | flops 268435456 | bytes 4980736 | tf_op jit(solution)/shard_map/spread_all/pallas_call | solution.py:130
  33.9 1.7 %copy.8 = f32[16,4096]{1,0:T(8,128)} copy(f32[16,4096]{1,0:T(8,128)} %spread_all.1) | data formatting | bytes 524288

commit v4 on v3

--- a/solution.py
+++ b/solution.py
@@ -13,10 +13,17 @@
 ORDER = (4, 5, 2, 3, 0, 1)
 ALPHA = 0.8
 CHUNKS = 4
+GROUP = 4
 
 
-def dot_nt(x, w):
-    turned = lax.dot_general(w, x, (((1,), (1,)), ((), ())), preferred_element_type=jnp.float32)
+def grouped(xs, ws):
+    zero = jnp.zeros_like(xs[0])
+    count = len(xs)
+    placed = [jnp.concatenate([xs[i] if k == i else zero for k in range(count)], axis=1)
+              for i in range(count)]
+    turned = lax.dot_general(
+        jnp.concatenate(ws, axis=1), jnp.concatenate(placed, axis=0),
+        (((1,), (1,)), ((), ())), preferred_element_type=jnp.float32)
     return turned.T
 
 
@@ -85,36 +92,44 @@
             for load in loads:
                 load.wait()
 
-        def first(r, carry):
-            acc_ref[r] = dot_nt(ext[r], w_ref[off_ref[0, r]])
+        def first(g, carry):
+            rows = [g * GROUP + i for i in range(GROUP)]
+            acc_ref[g] = grouped([ext[r] for r in rows], [w_ref[off_ref[0, r]] for r in rows])
             return carry
 
-        lax.fori_loop(0, nrb, first, 0, unroll=True)
+        lax.fori_loop(0, nrb // GROUP, first, 0, unroll=True)
 
         for copy in flying:
             copy.wait_recv()
 
-        def rest(r, carry):
-            begin, end = off_ref[0, r], off_ref[0, r + 1]
+        def rest(g, carry):
+            rows = [g * GROUP + i for i in range(GROUP)]
             xs, ws = [], []
-            for k in range(1, MAXR):
-                slot = jnp.minimum(begin + k, nnz - 1)
-                col = jnp.where(begin + k < end, col_ref[0, slot], none)
-                xs.append(ext[col])
-                ws.append(w_ref[slot])
-            total = acc_ref[r] + dot_nt(jnp.concatenate(xs, axis=1), jnp.concatenate(ws, axis=1))
-            cols = pl.ds(pl.multiple_of(r * blk, blk), blk)
-            scale = scale_ref[pl.ds(r, 1), :]
-            field = ALPHA * scale * total + (1.0 - ALPHA) * seeds_ref[:, cols]
-            if step == ITERS - 1:
-                out_ref[:, cols] = field
-            else:
-                scaled = (field * scale).astype(jnp.bfloat16)
-                own_ref[r] = scaled
-                ext_refs[step + 1][r] = scaled
+            for r in rows:
+                begin, end = off_ref[0, r], off_ref[0, r + 1]
+                x, w = [], []
+                for k in range(1, MAXR):
+                    slot = jnp.minimum(begin + k, nnz - 1)
+                    col = jnp.where(begin + k < end, col_ref[0, slot], none)
+                    x.append(ext[col])
+                    w.append(w_ref[slot])
+                xs.append(jnp.concatenate(x, axis=1))
+                ws.append(jnp.concatenate(w, axis=1))
+            totals = acc_ref[g] + grouped(xs, ws)
+            for i, r in enumerate(rows):
+                total = totals[i * width:(i + 1) * width]
+                cols = pl.ds(pl.multiple_of(r * blk, blk), blk)
+                scale = scale_ref[pl.ds(r, 1), :]
+                field = ALPHA * scale * total + (1.0 - ALPHA) * seeds_ref[:, cols]
+                if step == ITERS - 1:
+                    out_ref[:, cols] = field
+                else:
+                    scaled = (field * scale).astype(jnp.bfloat16)
+                    own_ref[r] = scaled
+                    ext_refs[step + 1][r] = scaled
             return carry
 
-        lax.fori_loop(0, nrb, rest, 0, unroll=True)
+        lax.fori_loop(0, nrb // GROUP, rest, 0, unroll=True)
 
     for copy in copies:
         copy.wait_send()
@@ -140,7 +155,7 @@
             pltpu.VMEM(seeds.shape, jnp.float32),
             pltpu.VMEM((nnz, blk, blk), jnp.bfloat16),
             pltpu.VMEM((nrb, width, blk), jnp.bfloat16),
-            pltpu.VMEM((nrb, width, blk), jnp.float32),
+            pltpu.VMEM((nrb // GROUP, GROUP * width, blk), jnp.float32),
             [pltpu.VMEM((nrb + parts * per + 1, width, blk), jnp.bfloat16) for _ in range(ITERS)],
             [pltpu.VMEM((parts * per, width, blk), jnp.bfloat16) for _ in range(ITERS)],
             pltpu.SemaphoreType.DMA((5,)),

time: 35.7 us -> 35.6 us (level)
  no operation moved by 1% of the time
where the time goes in v4:
time: 35.6 us; the launch traced here: 35.5 us
  Pallas kernels  33.8 us (95%)
  local copies, waits for them, and re-layouts  1.67 us (5%)
    pallas_call x1, Pallas kernels, on_device(): pl.pallas_call(functools.partial(kernel, n), out_shape=jax.ShapeDtypeStru...  33.8 us
    unnamed x1, local copies, waits for them, and re-layouts  1.67 us

profile of v4, /device:TPU:0, one launch (start us, length us, event | category | flops | bytes accessed | tf_op | source)
XLA Modules:
  0.0 35.5 jit_solution(4645327547927579245)
XLA Ops:
  0.0 33.8 %spread_all.1 = f32[16,4096]{1,0:T(8,128)} custom-call(s32[1,128]{1,0:T(1,128)} %col_hbm.1, s32[1,33]{1,0:T(1,128)} %off_hbm.1, s32[6,1,8]{2,1,0:T(1,128)} %bitcast.3, f32[32,128]{1,0:T(8,128)} %bitcast.2, f32[16,4096]{1,0:T(8,128)} %seeds_hbm.1, bf16[128,128,128]{2,1,0:T(8,128)(2,1)} %blocks_ref.1), custom_call_target="tpu_custom_call" | custom-call | flops 268435456 | bytes 4980736 | tf_op jit(solution)/shard_map/spread_all/pallas_call | solution.py:145
  33.8 1.7 %copy.8 = f32[16,4096]{1,0:T(8,128)} copy(f32[16,4096]{1,0:T(8,128)} %spread_all.1) | data formatting | bytes 524288

commit v5 on v3

--- a/solution.py
+++ b/solution.py
@@ -107,7 +107,7 @@
             scale = scale_ref[pl.ds(r, 1), :]
             field = ALPHA * scale * total + (1.0 - ALPHA) * seeds_ref[:, cols]
             if step == ITERS - 1:
-                out_ref[:, cols] = field
+                out_ref[:, cols] = total
             else:
                 scaled = (field * scale).astype(jnp.bfloat16)
                 own_ref[r] = scaled
@@ -127,7 +127,7 @@
     parts, per = send_index.shape[1], send_index.shape[2]
     n = lax.axis_size("dom")
     hbm = pl.BlockSpec(memory_space=pltpu.HBM)
-    return pl.pallas_call(
+    product = pl.pallas_call(
         functools.partial(kernel, n),
         out_shape=jax.ShapeDtypeStruct(seeds.shape, jnp.float32),
         in_specs=[hbm] * 6,
@@ -156,6 +156,7 @@
             transcendentals=0),
         name="spread_all",
     )(col_index, row_offsets, send_index.transpose(1, 0, 2), deg_scale.reshape(nrb, blk), seeds, blocks)
+    return ALPHA * deg_scale[None, :] * product + (1.0 - ALPHA) * seeds
 
 
 def solution(mesh):

time: 35.7 us -> 37.2 us (1.042)
  other arithmetic: 0 us -> 3.09 us
  local copies, waits for them, and re-layouts: 1.67 us -> 0 us
    add x0 -> x1, other arithmetic: none -> 1.77 us  [on_device(): return ALPHA * deg_scale[None, :] * product + (1.0 - ALPHA) * seeds]
    unnamed x1 -> x0, local copies, waits for them, and re-layouts: 1.67 us -> none
    mul x0 -> x1, other arithmetic: none -> 1.32 us  [on_device(): return ALPHA * deg_scale[None, :] * product + (1.0 - ALPHA) * seeds]
where the time goes in v5:
time: 37.2 us; the launch traced here: 37 us
  Pallas kernels  33.8 us (91%)
  other arithmetic  3.09 us (8%)
    pallas_call x1, Pallas kernels, on_device(): pl.pallas_call(functools.partial(kernel, n), out_shape=jax.ShapeDtypeStru...  33.8 us
    add x1, other arithmetic, on_device(): return ALPHA * deg_scale[None, :] * product + (1.0 - ALPHA) * seeds  1.77 us
    mul x1, other arithmetic, on_device(): return ALPHA * deg_scale[None, :] * product + (1.0 - ALPHA) * seeds  1.32 us

profile of v5, /device:TPU:0, one launch (start us, length us, event | category | flops | bytes accessed | tf_op | source)
XLA Modules:
  0.0 37.0 jit_solution(14117708423130407922)
XLA Ops:
  0.0 1.3 %broadcast_multiply_fusion = f32[4096]{0:T(1024)} fusion(f32[4096]{0:T(1024)} %param.10), kind=kLoop, calls=%fused_computation.1 | loop fusion | flops 4096 | bytes 32768 | tf_op jit(solution)/shard_map/mul | solution.py:159
  1.3 33.8 %spread_all.1 = f32[16,4096]{1,0:T(8,128)} custom-call(s32[1,128]{1,0:T(1,128)} %col_hbm.1, s32[1,33]{1,0:T(1,128)} %off_hbm.1, s32[6,1,8]{2,1,0:T(1,128)} %bitcast.3, f32[32,128]{1,0:T(8,128)} %bitcast.2, f32[16,4096]{1,0:T(8,128)} %seeds_hbm.1, bf16[128,128,128]{2,1,0:T(8,128)(2,1)} %blocks_ref.1), custom_call_target="tpu_custom_call" | custom-call | flops 268435456 | bytes 4980736 | tf_op jit(solution)/shard_map/spread_all/pallas_call | solution.py:130
  35.2 1.8 %multiply_add_fusion = f32[16,4096]{1,0:T(8,128)} fusion(f32[16,4096]{1,0:T(8,128)} %seeds_hbm.1, f32[16,4096]{1,0:T(8,128)} %spread_all.1, f32[4096]{0:T(1024)} %broadcast_multiply_fusion), kind=kLoop, calls=%fused_computation | loop fusion | flops 196608 | bytes 802816 | tf_op jit(solution)/shard_map/add | solution.py:159

commit v6 on v3

--- a/solution.py
+++ b/solution.py
@@ -20,9 +20,9 @@
     return turned.T
 
 
-def kernel(n, col_hbm, off_hbm, lists_hbm, scale_hbm, seeds_hbm, blocks_ref, out_ref,
+def kernel(n, col_hbm, off_hbm, lists_hbm, scale_hbm, seeds_hbm, blocks_ref, out_hbm,
            col_ref, off_ref, lists_ref, scale_ref, seeds_ref,
-           w_ref, own_ref, acc_ref, ext_refs, send_refs, in_sem, w_sem, send_sem, recv_sem):
+           out_ref, w_ref, own_ref, acc_ref, ext_refs, send_refs, out_sem, in_sem, w_sem, send_sem, recv_sem):
     nnz, blk = w_ref.shape[0], w_ref.shape[1]
     nrb, width = own_ref.shape[0], own_ref.shape[1]
     parts, per = lists_ref.shape[0], lists_ref.shape[2]
@@ -114,7 +114,19 @@
                 ext_refs[step + 1][r] = scaled
             return carry
 
-        lax.fori_loop(0, nrb, rest, 0, unroll=True)
+        if step < ITERS - 1:
+            lax.fori_loop(0, nrb, rest, 0, unroll=True)
+
+    results = []
+    part = nrb // CHUNKS
+    for c in range(CHUNKS):
+        lax.fori_loop(c * part, (c + 1) * part, rest, 0, unroll=True)
+        cols = pl.ds(c * part * blk, part * blk)
+        result = pltpu.make_async_copy(out_ref.at[:, cols], out_hbm.at[:, cols], out_sem.at[c])
+        result.start()
+        results.append(result)
+    for result in results:
+        result.wait()
 
     for copy in copies:
         copy.wait_send()
@@ -131,18 +143,20 @@
         functools.partial(kernel, n),
         out_shape=jax.ShapeDtypeStruct(seeds.shape, jnp.float32),
         in_specs=[hbm] * 6,
-        out_specs=pl.BlockSpec(memory_space=pltpu.VMEM),
+        out_specs=hbm,
         scratch_shapes=[
             pltpu.SMEM(col_index.shape, jnp.int32),
             pltpu.SMEM(row_offsets.shape, jnp.int32),
             pltpu.SMEM((parts, 1, per), jnp.int32),
             pltpu.VMEM((nrb, blk), jnp.float32),
             pltpu.VMEM(seeds.shape, jnp.float32),
+            pltpu.VMEM(seeds.shape, jnp.float32),
             pltpu.VMEM((nnz, blk, blk), jnp.bfloat16),
             pltpu.VMEM((nrb, width, blk), jnp.bfloat16),
             pltpu.VMEM((nrb, width, blk), jnp.float32),
             [pltpu.VMEM((nrb + parts * per + 1, width, blk), jnp.bfloat16) for _ in range(ITERS)],
             [pltpu.VMEM((parts * per, width, blk), jnp.bfloat16) for _ in range(ITERS)],
+            pltpu.SemaphoreType.DMA((CHUNKS,)),
             pltpu.SemaphoreType.DMA((5,)),
             pltpu.SemaphoreType.DMA((CHUNKS,)),
             pltpu.SemaphoreType.DMA((ITERS, parts)),

time: 35.7 us -> 35.6 us (level)
  no operation moved by 1% of the time
where the time goes in v6:
time: 35.6 us; the launch traced here: 35.5 us
  Pallas kernels  33.8 us (95%)
  local copies, waits for them, and re-layouts  1.67 us (5%)
    pallas_call x1, Pallas kernels, on_device(): pl.pallas_call(functools.partial(kernel, n), out_shape=jax.ShapeDtypeStru...  33.8 us
    unnamed x1, local copies, waits for them, and re-layouts  1.67 us

profile of v6, /device:TPU:0, one launch (start us, length us, event | category | flops | bytes accessed | tf_op | source)
XLA Modules:
  0.0 35.5 jit_solution(2491890364086331007)
XLA Ops:
  0.0 33.8 %spread_all.1 = f32[16,4096]{1,0:T(8,128)} custom-call(s32[1,128]{1,0:T(1,128)} %col_hbm.1, s32[1,33]{1,0:T(1,128)} %off_hbm.1, s32[6,1,8]{2,1,0:T(1,128)} %bitcast.3, f32[32,128]{1,0:T(8,128)} %bitcast.2, f32[16,4096]{1,0:T(8,128)} %seeds_hbm.1, bf16[128,128,128]{2,1,0:T(8,128)(2,1)} %blocks_ref.1), custom_call_target="tpu_custom_call" | custom-call | flops 268435456 | bytes 4980736 | tf_op jit(solution)/shard_map/spread_all/pallas_call | solution.py:142
  33.8 1.7 %copy.8 = f32[16,4096]{1,0:T(8,128)} copy(f32[16,4096]{1,0:T(8,128)} %spread_all.1) | data formatting | bytes 524288
